TPU v7x, 32 devices: a whole 2x2x4 slice. The times are simulated.
32 devices in a mesh: dp: 2 (over y), tm: 16 (over z, x, core).
Axes of the slice: x: 2, y: 2, z: 4, core: 2. Of those that a mesh axis runs over, the one named last changes fastest.
Arguments:
- query_proj: bfloat16 [2, 2048, 768], P('dp', 'tm'), may hold values from -240 to 240
- key_proj: bfloat16 [2, 2048, 768], P('dp', 'tm'), may hold values from -6 to 6
- value_proj: bfloat16 [2, 2048, 768], P('dp', 'tm'), may hold values from -6 to 6
- cotangent: bfloat16 [2, 2048, 768], P('dp', 'tm'), may hold values from -6 to 6
- lengths: int32 [2], P('dp'), may hold values from 1024 to 2048, as said below
- rel_bias: float32 [12, 257], replicated, may hold values from -4 to 4
Outputs:
- context: bfloat16 [2, 2048, 768], P('dp', 'tm')
- grad_query: bfloat16 [2, 2048, 768], P('dp', 'tm')
- grad_key: bfloat16 [2, 2048, 768], P('dp', 'tm')
- grad_value: bfloat16 [2, 2048, 768], P('dp', 'tm')
- grad_bias: float32 [12, 257], replicated
Inputs may be any that keep to these rules, and one draw needn't show every extreme that they name: `lengths`: one utterance has all 2048 frames valid and another exactly 1024.
All inputs are finite; a program needn't handle non-finite values.
Results may differ from a plain program's by a relative error of at most 0.005.
Values may be sent and summed in bfloat16 or wider, within the bound.
A program may use at most 64 MiB of HBM per device.

v0:
```python
import jax
import jax.numpy as jnp
from jax import lax
from jax.sharding import PartitionSpec as P

H = 12
HD = 64
W = 128


masked_score = -1e30


def padded_2(cells, sides, width):
    for axis, dim in sides:
        count = lax.axis_size(axis)
        ends = count - 1
        head = lax.slice_in_dim(cells, 0, width, axis=dim)
        tail = lax.slice_in_dim(cells, cells.shape[dim] - width, cells.shape[dim], axis=dim)
        cells = jnp.concatenate(
            [
                lax.ppermute(tail, axis, [(i, (i + 1) % count) for i in range(ends)]),
                cells,
                lax.ppermute(head, axis, [((i + 1) % count, i) for i in range(ends)]),
            ],
            axis=dim,
        )
    return cells


def band_matrix(bias_table, height, breadth):
    num_heads = bias_table.shape[0]
    span_cols = bias_table.shape[1]
    repeated = jnp.broadcast_to(bias_table[:, None, :], (num_heads, height, span_cols))
    padded = jnp.pad(repeated, ((0, 0), (0, 0), (0, breadth + 1 - span_cols)))
    flattened = padded.reshape(num_heads, height * (breadth + 1))[:, : height * breadth]
    return flattened.reshape(num_heads, height, breadth)


def band_sum(values, span_cols):
    num_heads, height, breadth = values.shape
    flattened = jnp.pad(values.reshape(num_heads, height * breadth), ((0, 0), (0, height)))
    return jnp.sum(flattened.reshape(num_heads, height, breadth + 1)[:, :, :span_cols], axis=1)


def heads_first(array, rows):
    return array.reshape(rows, H, HD).transpose(1, 0, 2)


def rows_first(array):
    num_heads, rows, size = array.shape
    return array.transpose(1, 0, 2).reshape(rows, num_heads * size)


def query_side(query_rows, key_rows, value_rows, grad_rows, bias_table, query_pos, key_pos, length):
    scaling = HD ** (-0.5)
    height = query_rows.shape[1]
    breadth = key_rows.shape[1]
    scores = (
        jnp.einsum("hqd,hkd->hqk", query_rows, key_rows, preferred_element_type=jnp.float32)
        * scaling
    )
    scores = scores + band_matrix(bias_table, height, breadth)
    allowed = (
        (jnp.abs(key_pos[None, :] - query_pos[:, None]) <= W)
        & (key_pos[None, :] >= 0)
        & (key_pos[None, :] < length)
    )
    scores = jnp.where(allowed[None], scores, masked_score)
    row_max = jnp.max(scores, axis=-1)
    shifted = jnp.exp(scores - row_max[..., None])
    row_total = jnp.sum(shifted, axis=-1)
    log_total = row_max + jnp.log(row_total)
    attn_probs = shifted / row_total[..., None]
    valid_rows = query_pos < length
    probs_low = attn_probs.astype(jnp.bfloat16)
    mixed = jnp.einsum("hqk,hkd->hqd", probs_low, value_rows, preferred_element_type=jnp.float32)
    context = jnp.where(valid_rows[None, :, None], mixed, 0.0).astype(jnp.bfloat16)
    masked_grad = jnp.where(valid_rows[None, :, None], grad_rows, jnp.zeros_like(grad_rows))
    grad_probs = jnp.einsum(
        "hqd,hkd->hqk", masked_grad, value_rows, preferred_element_type=jnp.float32
    )
    row_delta = jnp.sum(attn_probs * grad_probs, axis=-1)
    grad_scores = attn_probs * (grad_probs - row_delta[..., None])
    grad_low = grad_scores.astype(jnp.bfloat16)
    grad_query = (
        jnp.einsum("hqk,hkd->hqd", grad_low, key_rows, preferred_element_type=jnp.float32) * scaling
    ).astype(jnp.bfloat16)
    grad_table = band_sum(grad_scores, bias_table.shape[1])
    results = (context, grad_query, log_total, row_delta, grad_table)
    return results


def key_side(
    key_rows,
    value_rows,
    query_rows,
    grad_rows,
    log_total,
    row_delta,
    bias_table,
    key_pos,
    query_pos,
    length,
):
    scaling = HD ** (-0.5)
    height = key_rows.shape[1]
    breadth = query_rows.shape[1]
    scores = (
        jnp.einsum("hkd,hqd->hkq", key_rows, query_rows, preferred_element_type=jnp.float32)
        * scaling
    )
    scores = scores + band_matrix(bias_table[:, ::-1], height, breadth)
    valid_query = (query_pos >= 0) & (query_pos < length)
    allowed = (
        (jnp.abs(query_pos[None, :] - key_pos[:, None]) <= W)
        & (key_pos[:, None] < length)
        & valid_query[None, :]
    )
    attn_probs = jnp.where(
        allowed[None], jnp.exp(jnp.where(allowed[None], scores - log_total[:, None, :], 0.0)), 0.0
    )
    probs_low = attn_probs.astype(jnp.bfloat16)
    masked_grad = jnp.where(valid_query[None, :, None], grad_rows, jnp.zeros_like(grad_rows))
    grad_probs = jnp.einsum(
        "hkd,hqd->hkq", value_rows, masked_grad, preferred_element_type=jnp.float32
    )
    grad_scores = attn_probs * (grad_probs - row_delta[:, None, :])
    grad_low = grad_scores.astype(jnp.bfloat16)
    key_grad = (
        jnp.einsum("hkq,hqd->hkd", grad_low, query_rows, preferred_element_type=jnp.float32)
        * scaling
    )
    value_grad = jnp.einsum(
        "hkq,hqd->hkd", probs_low, masked_grad, preferred_element_type=jnp.float32
    )
    return (key_grad, value_grad)


def on_device(query_proj, key_proj, value_proj, cotangent, lengths, rel_bias):
    frames = query_proj.shape[1]
    model_width = query_proj.shape[2]
    extended = frames + 2 * W
    first_frame = lax.axis_index("tm") * frames
    query_pos = first_frame + jnp.arange(frames, dtype=jnp.int32)
    key_pos = first_frame - W + jnp.arange(extended, dtype=jnp.int32)
    length = lengths[0]
    head_group = 4
    groups = H // head_group
    with_rims = padded_2(jnp.stack([key_proj, value_proj, query_proj, cotangent]), (("tm", 2),), W)
    key_ext = heads_first(with_rims[0, 0], extended)
    value_ext = heads_first(with_rims[1, 0], extended)
    query_own = heads_first(query_proj[0], frames)
    grad_own = heads_first(cotangent[0], frames)
    outputs = []
    for group_index in range(groups):
        low_head = group_index * head_group
        high_head = low_head + head_group
        outputs.append(
            query_side(
                query_own[low_head:high_head],
                key_ext[low_head:high_head],
                value_ext[low_head:high_head],
                grad_own[low_head:high_head],
                rel_bias[low_head:high_head],
                query_pos,
                key_pos,
                length,
            )
        )
    context = rows_first(jnp.concatenate([item[0] for item in outputs], axis=0))
    grad_query = rows_first(jnp.concatenate([item[1] for item in outputs], axis=0))
    log_totals = jnp.concatenate([item[2] for item in outputs], axis=0)
    row_deltas = jnp.concatenate([item[3] for item in outputs], axis=0)
    grad_table = jnp.concatenate([item[4] for item in outputs], axis=0)
    row_stats_all = padded_2(jnp.stack([log_totals, row_deltas]), (("tm", 2),), W)
    query_ext = heads_first(with_rims[2, 0], extended)
    grad_ext = heads_first(with_rims[3, 0], extended)
    key_own = heads_first(key_proj[0], frames)
    value_own = heads_first(value_proj[0], frames)
    key_parts = []
    value_parts = []
    for group_index in range(groups):
        low_head = group_index * head_group
        high_head = low_head + head_group
        key_part, value_part = key_side(
            key_own[low_head:high_head],
            value_own[low_head:high_head],
            query_ext[low_head:high_head],
            grad_ext[low_head:high_head],
            row_stats_all[0, low_head:high_head],
            row_stats_all[1, low_head:high_head],
            rel_bias[low_head:high_head],
            query_pos,
            key_pos,
            length,
        )
        key_parts.append(key_part)
        value_parts.append(value_part)
    grad_key = rows_first(jnp.concatenate(key_parts, axis=0)).astype(jnp.bfloat16)
    grad_value = rows_first(jnp.concatenate(value_parts, axis=0)).astype(jnp.bfloat16)
    grad_bias = lax.psum(grad_table, ("dp", "tm"))
    return (
        context.reshape(1, frames, model_width),
        grad_query.reshape(1, frames, model_width),
        grad_key.reshape(1, frames, model_width),
        grad_value.reshape(1, frames, model_width),
        grad_bias,
    )


def solution(mesh):
    return jax.shard_map(
        on_device,
        mesh=mesh,
        in_specs=(
            P("dp", "tm", None),
            P("dp", "tm", None),
            P("dp", "tm", None),
            P("dp", "tm", None),
            P("dp"),
            P(),
        ),
        out_specs=(
            P("dp", "tm", None),
            P("dp", "tm", None),
            P("dp", "tm", None),
            P("dp", "tm", None),
            P(),
        ),
        check_vma=False,
    )
```

profile of v0, /device:TPU:0, one launch (start us, length us, event | category | flops | bytes accessed | tf_op | source)
XLA Modules:
  0.0 117.3 jit_solution(791555056097660915)
XLA Ops:
  0.6 1.1 copy.43
  1.8 1.2 copy.42
  2.9 1.1 copy.41
  4.0 1.1 copy.40
  5.1 1.0 pad_maximum_fusion.1
  6.1 1.3 %collective-permute-start.1 = (bf16[4,1,128,768]{2,3,1,0:T(8,128)(2,1)}, bf16[4,1,128,768]{2,3,1,0:T(8,128)(2,1)}, u32[]{:S(2)}, u32[]{:S(2)}) collective-permute-start(bf16[4,1,128,768]{2,3,1,0:T(8,128)(2,1)} %pad_maximum_fusion.1), channel_id=1, source_target_pairs={{1,0},{2,1},{3,2},{4,3},{5,4},{6,5},{7,6},{8,7},{9,8},{10,9},{11,1... | collective-permute-start | bytes 2359304 | tf_op jit(solution)/shard_map/ppermute | solution.py:24
  7.4 4.0 %collective-permute-start = (bf16[4,1,128,768]{2,3,1,0:T(8,128)(2,1)}, bf16[4,1,128,768]{2,3,1,0:T(8,128)(2,1)}, u32[]{:S(2)}, u32[]{:S(2)}) collective-permute-start(bf16[4,1,128,768]{2,3,1,0:T(8,128)(2,1)} %pad_maximum_fusion.1), channel_id=1, source_target_pairs={{0,1},{1,2},{2,3},{3,4},{4,5},{5,6},{6,7},{7,8},{8,9},{9,10},{10,1... | collective-permute-start | bytes 2359304 | tf_op jit(solution)/shard_map/ppermute | solution.py:22
  12.2 1.0 reshape.263
  13.8 1.0 reshape.261
  15.0 1.1 copy.47
  16.3 1.0 reshape.259
  17.5 1.2 copy.45
  19.2 1.0 reshape.269
  20.4 1.2 %copy.67 = f32[4,128,384]{1,2,0:T(8,128)} copy(f32[4,128,384]{2,1,0:T(8,128)S(1)} %bitcast.189) | data formatting | bytes 1572864 | tf_op jit(solution)/shard_map/reshape | solution.py:37
  22.1 1.0 reshape.267
  23.3 1.2 copy.65
  25.0 1.0 reshape.265
  26.1 1.2 copy.62
  27.3 0.9 and_and_fusion
  28.2 1.6 %pad_maximum_fusion = bf16[4,1,384,768]{2,3,1,0:T(8,128)(2,1)S(1)} fusion(bf16[4,1,128,768]{2,3,1,0:T(8,128)(2,1)} %collective-permute-done.1, bf16[1,1,128,768]{2,3,1,0:T(8,128)(2,1)S(1)} %bitcast.213, bf16[1,1,128,768]{2,3,1,0:T(8,128)(2,1)S(1)} %bitcast.174, bf16[1,1,128,768]{2,3,1,0:T(8,128)(2,1)S(1)} %bitcast.203, ...), kind=kLoop, calls=%fused_computation | loop fusion | flops 14155776 | bytes 4718592 | tf_op jit(solution)/shard_map/concatenate | solution.py:20
  29.8 1.3 %fusion.128 = (bf16[1,1,384,768]{2,3,1,0:T(8,128)(2,1)}, bf16[1,1,384,768]{2,3,1,0:T(8,128)(2,1)}, bf16[1,1,384,768]{2,3,1,0:T(8,128)(2,1)S(1)}, bf16[1,1,384,768]{2,3,1,0:T(8,128)(2,1)S(1)}) fusion(bf16[4,1,384,768]{2,3,1,0:T(8,128)(2,1)S(1)} %pad_maximum_fusion), kind=kLoop, calls=%fused_computation.181 | loop fusion | bytes 4718592 | tf_op jit(solution)/shard_map/slice | solution.py:178
  31.1 0.3 fusion.130
  31.5 0.3 fusion.131
  32.0 0.3 fusion.29
  32.4 0.9 fusion.28
  33.3 0.3 multiply_reduce_fusion
  33.7 1.2 %multiply_reduce_fusion.1 = (f32[4,128]{1,0:T(4,128)S(1)}, f32[4,128,384]{1,2,0:T(8,128)}) fusion(f32[4,128]{1,0:T(4,128)S(1)} %fusion.42, f32[4,128,384]{1,2,0:T(8,128)S(1)} %get-tuple-element.35, f32[4,128]{1,0:T(4,128)S(1)} %get-tuple-element.34, bf16[12,384,64]{1,2,0:T(8,128)(2,1)S(1)} %bitcast.230, bf16[12,128,64]{1,2,0:T(8,128)(2,1)S(1)} %bitcast.215, ...), kind=kOutput, calls=%fused_computation.74 | convolution fusion | flops 25984512 | bytes 1841664 | tf_op jit(solution)/shard_map/hqd,hkd->hqk/dot_general | solution.py:80
  34.9 0.4 fusion.132
  35.4 0.9 fusion.27
  36.3 1.2 %multiply_reduce_fusion.2 = (f32[4,128]{1,0:T(4,128)S(1)}, f32[4,128,384]{1,2,0:T(8,128)}) fusion(f32[4,128]{1,0:T(4,128)S(1)} %fusion.40, f32[4,128,384]{1,2,0:T(8,128)S(1)} %get-tuple-element.37, f32[4,128]{1,0:T(4,128)S(1)} %get-tuple-element.36, bf16[12,384,64]{1,2,0:T(8,128)(2,1)S(1)} %bitcast.232, bf16[12,128,64]{1,2,0:T(8,128)(2,1)S(1)} %bitcast.216, ...), kind=kOutput, calls=%fused_computation.76 | convolution fusion | flops 25984512 | bytes 1841664 | tf_op jit(solution)/shard_map/hqd,hkd->hqk/dot_general | solution.py:80
  37.6 0.5 copy-done.21
  38.1 0.6 pad_maximum_fusion.7
  38.7 1.3 %collective-permute-start.3 = (f32[2,12,128]{2,1,0:T(8,128)}, f32[2,12,128]{2,1,0:T(8,128)S(1)}, u32[]{:S(2)}, u32[]{:S(2)}) collective-permute-start(f32[2,12,128]{2,1,0:T(8,128)} %pad_maximum_fusion.7), channel_id=1, source_target_pairs={{1,0},{2,1},{3,2},{4,3},{5,4},{6,5},{7,6},{8,7},{9,8},{10,9},{11,1... | collective-permute-start | bytes 36872 | tf_op jit(solution)/shard_map/ppermute | solution.py:24
  40.0 4.3 %collective-permute-start.2 = (f32[2,12,128]{2,1,0:T(8,128)}, f32[2,12,128]{2,1,0:T(8,128)S(1)}, u32[]{:S(2)}, u32[]{:S(2)}) collective-permute-start(f32[2,12,128]{2,1,0:T(8,128)} %pad_maximum_fusion.7), channel_id=1, source_target_pairs={{0,1},{1,2},{2,3},{3,4},{4,5},{5,6},{6,7},{7,8},{8,9},{9,10},{10,1... | collective-permute-start | bytes 36872 | tf_op jit(solution)/shard_map/ppermute | solution.py:22
  44.8 1.2 copy.74
  45.9 1.3 %subtract_multiply_fusion.1 = f32[4,128,384]{1,2,0:T(8,128)S(1)} fusion(f32[4,128,384]{1,2,0:T(8,128)} %get-tuple-element.41, f32[4,128]{1,0:T(4,128)S(1)} %copy-done.20, f32[4,128]{1,0:T(4,128)S(1)} %fusion.42, f32[4,128,384]{1,2,0:T(8,128)S(1)} %get-tuple-element.35, f32[4,128]{1,0:T(4,128)S(1)} %get-tuple-element.34), kind=kLoop, calls=%fused_computation.73 | loop fusion | flops 786432 | bytes 2365440 | tf_op jit(solution)/shard_map/mul | solution.py:84
  47.2 0.8 fusion.31
  48.1 1.1 copy.73
  49.2 1.4 %subtract_multiply_fusion.2 = f32[4,128,384]{1,2,0:T(8,128)S(1)} fusion(f32[4,128,384]{1,2,0:T(8,128)} %get-tuple-element.43, f32[4,128]{1,0:T(4,128)S(1)} %copy-done.22, f32[4,128]{1,0:T(4,128)S(1)} %fusion.40, f32[4,128,384]{1,2,0:T(8,128)S(1)} %get-tuple-element.37, f32[4,128]{1,0:T(4,128)S(1)} %get-tuple-element.36), kind=kLoop, calls=%fused_computation.75 | loop fusion | flops 786432 | bytes 2365440 | tf_op jit(solution)/shard_map/mul | solution.py:84
  50.6 0.8 fusion.30
  51.4 1.2 copy.72
  52.6 0.5 copy.102
  53.3 1.0 reshape.276
  54.3 0.7 slice_reduce_fusion
  55.0 0.5 copy.101
  55.6 1.0 reshape.274
  56.7 0.7 slice_reduce_fusion.1
  57.4 0.5 copy.100
  58.0 1.0 reshape.272
  59.2 0.9 pad_maximum_fusion.2
  60.1 0.9 pad_maximum_fusion.3
  61.0 0.7 pad_maximum_fusion.6
  61.7 0.8 copy.75
  62.5 0.8 copy.76
  63.4 42.9 %psum.7 = f32[12,257]{1,0:T(8,128)} all-reduce(f32[12,257]{1,0:T(8,128)S(1)} %pad_maximum_fusion.6), channel_id=1, replica_groups=mesh['dp'=2,'tm'=16] {'dp','tm'}, use_global_device_ids=true, to_apply=%region_12.13 | all-reduce | flops 3084 | bytes 24672 | tf_op jit(solution)/shard_map/psum | solution.py:202
  106.4 1.5 %fusion.5 = f32[4,128,384]{1,2,0:T(8,128)S(1)} fusion(f32[4,128,384]{1,2,0:T(8,128)S(1)} %copy-done.8, bf16[12,384,64]{1,2,0:T(8,128)(2,1)} %bitcast.221, f32[4,384]{1,0:T(4,128)S(1)} %get-tuple-element.22, pred[128,384]{0,1:T(8,128)(4,1)} %get-tuple-element.30, bf16[12,128,64]{1,2,0:T(8,128)(2,1)S(1)} %bitcast.209), kind=kOutput, calls=%fused_computation.7 | convolution fusion | flops 26148864 | bytes 2283520 | tf_op jit(solution)/shard_map/hkd,hqd->hkq/dot_general | solution.py:110
  107.9 0.4 fusion.11
  108.3 0.4 copy-done.11
  109.2 1.8 %fusion.35 = bf16[4,128,64]{1,2,0:T(8,128)(2,1)S(1)} fusion(f32[4,128,384]{1,2,0:T(8,128)} %copy-done.11, f32[4,384]{1,0:T(4,128)S(1)} %get-tuple-element.26, bf16[12,384,64]{1,2,0:T(8,128)(2,1)} %bitcast.222, bf16[12,384,64]{1,2,0:T(8,128)(2,1)S(1)} %bitcast.198, pred[384]{0:T(512)(128)(4,1)S(1)} %copy-done.18, bf16[12,128,64]{1,2,0:T(8,128)(2,1)S(1)} %bitcast.204), kind=kOutput, calls=%fused_computation.51 | convolution fusion | flops 51085312 | bytes 1317376 | tf_op jit(solution)/shard_map/hkq,hqd->hkd/dot_general | solution.py:131
  111.0 1.5 %fusion.34 = bf16[4,128,64]{1,2,0:T(8,128)(2,1)S(1)} fusion(f32[4,128,384]{1,2,0:T(8,128)S(1)} %fusion.11, f32[4,384]{1,0:T(4,128)S(1)} %get-tuple-element.23, bf16[12,384,64]{1,2,0:T(8,128)(2,1)} %bitcast.223, bf16[12,384,64]{1,2,0:T(8,128)(2,1)S(1)} %bitcast.199, pred[384]{0:T(512)(128)(4,1)S(1)} %copy-done.18, bf16[12,128,64]{1,2,0:T(8,128)(2,1)S(1)} %bitcast.205), kind=kOutput, calls=%fused_computation.50 | convolution fusion | flops 51085312 | bytes 1317376 | tf_op jit(solution)/shard_map/hkq,hqd->hkd/dot_general | solution.py:131
  112.5 1.4 %fusion.17 = f32[4,128,384]{1,2,0:T(8,128)S(1)} fusion(f32[4,128,384]{1,2,0:T(8,128)S(1)} %copy-done.9, bf16[12,384,64]{1,2,0:T(8,128)(2,1)} %bitcast.224, f32[4,384]{1,0:T(4,128)S(1)} %get-tuple-element.25, pred[128,384]{0,1:T(8,128)(4,1)S(1)} %copy-done.15, bf16[12,128,64]{1,2,0:T(8,128)(2,1)S(1)} %bitcast.211), kind=kOutput, calls=%fused_computation.21 | convolution fusion | flops 26148864 | bytes 2283520 | tf_op jit(solution)/shard_map/hkd,hqd->hkq/dot_general | solution.py:110
  114.1 1.5 %fusion.33 = bf16[4,128,64]{1,2,0:T(8,128)(2,1)S(1)} fusion(f32[4,128,384]{1,2,0:T(8,128)S(1)} %fusion.17, f32[4,384]{1,0:T(4,128)S(1)} %get-tuple-element.21, bf16[12,384,64]{1,2,0:T(8,128)(2,1)} %bitcast.225, bf16[12,384,64]{1,2,0:T(8,128)(2,1)S(1)} %bitcast.201, pred[384]{0:T(512)(128)(4,1)S(1)} %copy-done.18, bf16[12,128,64]{1,2,0:T(8,128)(2,1)S(1)} %bitcast.206), kind=kOutput, calls=%fused_computation.49 | convolution fusion | flops 51085312 | bytes 1317376 | tf_op jit(solution)/shard_map/hkq,hqd->hkd/dot_general | solution.py:131
  115.6 0.8 copy.77
  116.4 0.8 copy.78
  (105 shorter events, 5.1 us)
Async XLA Ops:
  0.6 10.7 %copy-start.16 = (f32[12,257]{1,0:T(8,128)S(1)}, f32[12,257]{1,0:T(8,128)}, u32[]{:S(2)}) copy-start(f32[12,257]{1,0:T(8,128)} %param.11) | copy-start | bytes 37012
  1.7 26.5 %copy-start.6 = (bf16[1,128,768]{1,2,0:T(8,128)(2,1)}, bf16[1,128,768]{1,2,0:T(8,128)(2,1)S(1)}, u32[]{:S(2)}) copy-start(bf16[1,128,768]{1,2,0:T(8,128)(2,1)S(1)} %copy.43) | copy-start | bytes 589828
  6.1 22.1 %collective-permute-start.1 = (bf16[4,1,128,768]{2,3,1,0:T(8,128)(2,1)}, bf16[4,1,128,768]{2,3,1,0:T(8,128)(2,1)}, u32[]{:S(2)}, u32[]{:S(2)}) collective-permute-start(bf16[4,1,128,768]{2,3,1,0:T(8,128)(2,1)} %pad_maximum_fusion.1), channel_id=1, source_target_pairs={{1,0},{2,1},{3,2},{4,3},{5,4},{6,5},{7,6},{8,7},{9,8},{10,9},{11,1... | collective-permute-start | bytes 2359304 | tf_op jit(solution)/shard_map/ppermute | solution.py:24
  7.4 20.8 %collective-permute-start = (bf16[4,1,128,768]{2,3,1,0:T(8,128)(2,1)}, bf16[4,1,128,768]{2,3,1,0:T(8,128)(2,1)}, u32[]{:S(2)}, u32[]{:S(2)}) collective-permute-start(bf16[4,1,128,768]{2,3,1,0:T(8,128)(2,1)} %pad_maximum_fusion.1), channel_id=1, source_target_pairs={{0,1},{1,2},{2,3},{3,4},{4,5},{5,6},{6,7},{7,8},{8,9},{9,10},{10,1... | collective-permute-start | bytes 2359304 | tf_op jit(solution)/shard_map/ppermute | solution.py:22
  27.3 0.9 copy-start.17
  29.8 1.7 %copy-start.1 = (f32[4,128,384]{1,2,0:T(8,128)S(1)}, f32[4,128,384]{1,2,0:T(8,128)}, u32[]{:S(2)}) copy-start(f32[4,128,384]{1,2,0:T(8,128)} %copy.47) | copy-start | bytes 2359300
  32.3 1.1 copy-start.7
  33.7 1.2 %copy-start = (f32[4,128,384]{1,2,0:T(8,128)S(1)}, f32[4,128,384]{1,2,0:T(8,128)}, u32[]{:S(2)}) copy-start(f32[4,128,384]{1,2,0:T(8,128)} %copy.45) | copy-start | bytes 2359300
  34.9 2.7 %copy-start.19 = (f32[4,128]{1,0:T(4,128)}, f32[4,128]{1,0:T(4,128)S(1)}, u32[]{:S(2)}) copy-start(f32[4,128]{1,0:T(4,128)S(1)} %get-tuple-element.40) | copy-start | bytes 6148
  37.5 0.6 copy-start.21
  38.7 67.6 %collective-permute-start.3 = (f32[2,12,128]{2,1,0:T(8,128)}, f32[2,12,128]{2,1,0:T(8,128)S(1)}, u32[]{:S(2)}, u32[]{:S(2)}) collective-permute-start(f32[2,12,128]{2,1,0:T(8,128)} %pad_maximum_fusion.7), channel_id=1, source_target_pairs={{1,0},{2,1},{3,2},{4,3},{5,4},{6,5},{7,6},{8,7},{9,8},{10,9},{11,1... | collective-permute-start | bytes 36872 | tf_op jit(solution)/shard_map/ppermute | solution.py:24
  40.0 66.3 %collective-permute-start.2 = (f32[2,12,128]{2,1,0:T(8,128)}, f32[2,12,128]{2,1,0:T(8,128)S(1)}, u32[]{:S(2)}, u32[]{:S(2)}) collective-permute-start(f32[2,12,128]{2,1,0:T(8,128)} %pad_maximum_fusion.7), channel_id=1, source_target_pairs={{0,1},{1,2},{2,3},{3,4},{4,5},{5,6},{6,7},{7,8},{8,9},{9,10},{10,1... | collective-permute-start | bytes 36872 | tf_op jit(solution)/shard_map/ppermute | solution.py:22
  44.4 1.6 %copy-start.20 = (f32[4,128]{1,0:T(4,128)S(1)}, f32[4,128]{1,0:T(4,128)}, u32[]{:S(2)}) copy-start(f32[4,128]{1,0:T(4,128)} %copy-done.19) | copy-start | bytes 6148
  45.9 3.3 %copy-start.22 = (f32[4,128]{1,0:T(4,128)S(1)}, f32[4,128]{1,0:T(4,128)}, u32[]{:S(2)}) copy-start(f32[4,128]{1,0:T(4,128)} %copy-done.21) | copy-start | bytes 6148
  49.2 3.4 %copy-start.2 = (f32[4,128,384]{2,1,0:T(8,128)S(1)}, f32[4,128,384]{2,1,0:T(8,128)}, u32[]{:S(2)}) copy-start(f32[4,128,384]{2,1,0:T(8,128)} %copy.74) | copy-start | bytes 2359300
  53.1 1.9 %copy-start.3 = (f32[4,128,384]{2,1,0:T(8,128)S(1)}, f32[4,128,384]{2,1,0:T(8,128)}, u32[]{:S(2)}) copy-start(f32[4,128,384]{2,1,0:T(8,128)} %copy.73) | copy-start | bytes 2359300
  55.5 1.9 %copy-start.4 = (f32[4,128,384]{2,1,0:T(8,128)S(1)}, f32[4,128,384]{2,1,0:T(8,128)}, u32[]{:S(2)}) copy-start(f32[4,128,384]{2,1,0:T(8,128)} %copy.72) | copy-start | bytes 2359300
  57.9 1.3 %copy-start.13 = (bf16[4,128,64]{1,2,0:T(8,128)(2,1)S(1)}, bf16[4,128,64]{1,2,0:T(8,128)(2,1)}, u32[]{:S(2)}) copy-start(bf16[4,128,64]{1,2,0:T(8,128)(2,1)} %fusion.28) | copy-start | bytes 196612
  58.0 48.3 %copy-start.8 = (f32[4,128,384]{1,2,0:T(8,128)S(1)}, f32[4,128,384]{1,2,0:T(8,128)}, u32[]{:S(2)}) copy-start(f32[4,128,384]{1,2,0:T(8,128)} %copy.67) | copy-start | bytes 2359300
  59.0 48.8 %copy-start.10 = (f32[4,128,384]{1,2,0:T(8,128)S(1)}, f32[4,128,384]{1,2,0:T(8,128)}, u32[]{:S(2)}) copy-start(f32[4,128,384]{1,2,0:T(8,128)} %copy.65) | copy-start | bytes 2359300
  59.2 48.7 %copy-start.14 = (pred[128,384]{0,1:T(8,128)(4,1)S(1)}, pred[128,384]{0,1:T(8,128)(4,1)}, u32[]{:S(2)}) copy-start(pred[128,384]{0,1:T(8,128)(4,1)} %get-tuple-element.30) | copy-start | bytes 147460
  106.3 1.6 %copy-start.12 = (bf16[1,1,384,768]{2,3,1,0:T(8,128)(2,1)S(1)}, bf16[1,1,384,768]{2,3,1,0:T(8,128)(2,1)}, u32[]{:S(2)}) copy-start(bf16[1,1,384,768]{2,3,1,0:T(8,128)(2,1)} %get-tuple-element.18) | copy-start | bytes 1769476
  106.3 2.4 %copy-start.5 = (bf16[1,1,384,768]{2,3,1,0:T(8,128)(2,1)S(1)}, bf16[1,1,384,768]{2,3,1,0:T(8,128)(2,1)}, u32[]{:S(2)}) copy-start(bf16[1,1,384,768]{2,3,1,0:T(8,128)(2,1)} %get-tuple-element.17) | copy-start | bytes 1769476
  106.3 2.4 %copy-start.18 = (pred[384]{0:T(512)(128)(4,1)S(1)}, pred[384]{0:T(512)(128)(4,1)}, u32[]{:S(2)}) copy-start(pred[384]{0:T(512)(128)(4,1)} %copy-done.17) | copy-start | bytes 1156
  107.8 0.9 copy-start.11
  108.7 3.7 %copy-start.9 = (f32[4,128,384]{1,2,0:T(8,128)S(1)}, f32[4,128,384]{1,2,0:T(8,128)}, u32[]{:S(2)}) copy-start(f32[4,128,384]{1,2,0:T(8,128)} %copy.62) | copy-start | bytes 2359300
  108.8 3.7 %copy-start.15 = (pred[128,384]{0,1:T(8,128)(4,1)S(1)}, pred[128,384]{0,1:T(8,128)(4,1)}, u32[]{:S(2)}) copy-start(pred[128,384]{0,1:T(8,128)(4,1)} %get-tuple-element.30) | copy-start | bytes 147460
where the time goes:
time: 118 us; the launch traced here: 117 us
  blocking collectives  42.9 us (36%)
  local copies, waits for them, and re-layouts  33.6 us (28%)
  matrix products  16.5 us (14%)
  other arithmetic  11.4 us (10%)
  starting transfers between devices  10.9 us (9%)
  between operations  2.01 us (2%)
    psum x1, blocking collectives, on_device(): grad_bias = lax.psum(grad_table, ('dp', 'tm'))  42.9 us
    unnamed x69, local copies, waits for them, and re-layouts  11.7 us
    ppermute x2, starting transfers between devices, padded_2(): lax.ppermute(tail, axis, [(i, (i + 1) % count) for i in range(ends)])  8.32 us
    reshape x6, local copies, waits for them, and re-layouts, band_matrix(): padded.reshape(num_heads, height * (breadth + 1))[:, :height * breadth]  6.24 us
    reshape x6, local copies, waits for them, and re-layouts, band_matrix(): return flattened.reshape(num_heads, height, breadth)  6.07 us
    dot_general x3, matrix products, key_side(): jnp.einsum('hkq,hqd->hkd', grad_low, query_rows, preferred_element_type=j...  4.69 us
    mul x3, local copies, waits for them, and re-layouts, query_side(): grad_scores = attn_probs * (grad_probs - row_delta[..., None])  3.46 us
    dot_general x3, matrix products, key_side(): jnp.einsum('hkd,hqd->hkq', key_rows, query_rows, preferred_element_type=j...  3.28 us
  transfers between devices with their start and end apart: 4, of which 0 were waited for; matrix products, arithmetic and copies ran while one was open for 30% of the time, Pallas kernels for 0%

commit v1 on v0

v1 whole, which is shorter than its diff:
```python
import functools

import jax
import jax.numpy as jnp
from jax import lax
from jax.experimental import pallas as pl
from jax.experimental.pallas import tpu as pltpu
from jax.sharding import PartitionSpec as P

MESH = pl.DeviceIdType.MESH
masked_score = -1e30
lane_tile = 128
radix = 4


def sum_stages(n_dp, n_tm):
    stages = []
    stride = 1
    with_dp = True
    while stride < n_tm or with_dp:
        size = min(radix, n_tm // stride)
        stages.append((stride, size, with_dp))
        stride *= size
        with_dp = False
    return stages


def contract(left, right, left_dim, right_dim):
    return lax.dot_general(
        left, right, (((left_dim,), (right_dim,)), ((), ())), preferred_element_type=jnp.float32
    )


def kernel(
    plan,
    length_ref,
    bias_ref,
    query_hbm,
    key_hbm,
    value_hbm,
    grad_hbm,
    context_hbm,
    dquery_hbm,
    dkey_hbm,
    dvalue_hbm,
    dbias_ref,
    ext,
    own,
    bias_rows,
    bias_full,
    staged,
    key_sums,
    back_send,
    back_recv,
    diag_sums,
    tables,
    load_sem,
    store_sem,
    fwd_send_sem,
    fwd_recv_sem,
    back_send_sem,
    back_recv_sem,
    table_send_sem,
    table_recv_sem,
):
    n_dp, n_tm, heads, frames, head_size, span, chunks, chunk_lanes = plan
    extended = 3 * frames
    stages = sum_stages(n_dp, n_tm)
    dp = lax.axis_index("dp")
    tm = lax.axis_index("tm")
    has_left = tm > 0
    has_right = tm < n_tm - 1
    scaling = head_size ** (-0.5)

    def when_side(side, run):
        pl.when(has_left if side == 0 else has_right)(run)

    loads = [
        pltpu.make_async_copy(query_hbm.at[0], own.at[0], load_sem.at[0]),
        pltpu.make_async_copy(grad_hbm.at[0], own.at[1], load_sem.at[1]),
        pltpu.make_async_copy(key_hbm.at[0], ext.at[0, pl.ds(frames, frames)], load_sem.at[2]),
        pltpu.make_async_copy(value_hbm.at[0], ext.at[1, pl.ds(frames, frames)], load_sem.at[3]),
    ]
    for copy in loads:
        copy.start()

    def group_of(stage):
        stride, size, with_dp = stage
        place = lax.rem(lax.div(tm, stride), size)
        base = tm - place * stride
        total = size * (n_dp if with_dp else 1)
        mine = dp * size + place if with_dp else place

        def device(slot):
            other_dp = lax.div(slot, size) if with_dp else dp
            return (other_dp, base + lax.rem(slot, size) * stride)

        others = [lax.rem(mine + step, total) for step in range(1, total)]
        return mine, others, device, total

    groups = [group_of(stage) for stage in stages]

    barrier = pltpu.get_barrier_semaphore()

    def greet_left():
        pl.semaphore_signal(barrier, inc=1, device_id=(dp, tm - 1), device_id_type=MESH)

    def greet_right():
        pl.semaphore_signal(barrier, inc=1, device_id=(dp, tm + 1), device_id_type=MESH)

    when_side(0, greet_left)
    when_side(1, greet_right)
    greeted = 0
    for mine, others, device, total in groups:
        for slot in others:
            pl.semaphore_signal(barrier, inc=1, device_id=device(slot), device_id_type=MESH)
            greeted += 1
    neighbours = jnp.where(has_left, 1, 0) + jnp.where(has_right, 1, 0)
    pl.semaphore_wait(barrier, greeted + neighbours)

    def lanes(chunk):
        return pl.ds(chunk * chunk_lanes, chunk_lanes)

    def rim_copy(side, array, chunk):
        source = (key_hbm, value_hbm)[array].at[0, :, lanes(chunk)]
        target = ext.at[array, pl.ds(2 * frames * side, frames), lanes(chunk)]
        return pltpu.make_async_remote_copy(
            src_ref=source,
            dst_ref=target,
            send_sem=fwd_send_sem.at[side, array, chunk],
            recv_sem=fwd_recv_sem.at[side, array, chunk],
            device_id=(dp, tm + 1 - 2 * side),
            device_id_type=MESH,
        )

    def back_copy(side, chunk):
        return pltpu.make_async_remote_copy(
            src_ref=back_send.at[side, chunk],
            dst_ref=back_recv.at[side, chunk],
            send_sem=back_send_sem.at[side, chunk],
            recv_sem=back_recv_sem.at[side, chunk],
            device_id=(dp, tm - 1 + 2 * side),
            device_id_type=MESH,
        )

    for chunk in range(chunks):
        for array in (0, 1):
            for side in (0, 1):
                when_side(1 - side, lambda: rim_copy(side, array, chunk).start())

    def clear(side):
        rim = pl.ds(2 * frames * side, frames)
        for array in (0, 1):
            ext[array, rim, :] = jnp.zeros((frames, ext.shape[2]), ext.dtype)
        back_recv[1 - side] = jnp.zeros(back_recv.shape[1:], back_recv.dtype)

    pl.when(jnp.logical_not(has_left))(lambda: clear(0))
    pl.when(jnp.logical_not(has_right))(lambda: clear(1))

    length = length_ref[0]
    first = tm * frames
    row = lax.broadcasted_iota(jnp.int32, (frames, extended), 0)
    column = lax.broadcasted_iota(jnp.int32, (frames, extended), 1)
    offset = column - row
    key_pos = first - frames + column
    allowed = (offset >= 0) & (offset < span) & (key_pos >= 0) & (key_pos < length)
    bias_rows[...] = jnp.zeros_like(bias_rows)
    bias_rows[pl.ds(0, heads), pl.ds(0, span)] = bias_ref[...]
    for head in range(heads):
        spread = jnp.broadcast_to(bias_rows[pl.ds(head, 1), :], (frames, extended))
        rolled = pltpu.roll(spread, 0, 1, stride=1, stride_axis=0)
        bias_full[head] = jnp.where(allowed, rolled, masked_score)

    query_row = lax.broadcasted_iota(jnp.int32, (frames, lane_tile), 0)
    lane = lax.broadcasted_iota(jnp.int32, (frames, lane_tile), 1)
    valid = first + query_row < length
    valid_low = jnp.where(valid, 1.0, 0.0).astype(jnp.bfloat16)
    per_tile = lane_tile // head_size
    lane_head = lax.div(lane, head_size)
    picks = [jnp.where(lane_head == sub, 1.0, 0.0).astype(jnp.bfloat16) for sub in range(per_tile)]

    for copy in loads:
        copy.wait()

    stores = []

    def store(index, source, target):
        copy = pltpu.make_async_copy(source, target, store_sem.at[index])
        copy.start()
        stores.append(copy)

    for chunk in range(chunks):
        for array in (0, 1):
            for side in (0, 1):
                when_side(side, lambda: rim_copy(side, array, chunk).wait_recv())
        for tile in range(chunk_lanes // lane_tile):
            start = chunk * chunk_lanes + tile * lane_tile
            cols = pl.ds(start, lane_tile)
            first_head = start // head_size
            query = own[0, :, cols]
            grad = own[1, :, cols] * valid_low
            key = ext[0, :, cols]
            value = ext[1, :, cols]
            queries = jnp.concatenate([query * pick for pick in picks], axis=0)
            grads = jnp.concatenate([grad * pick for pick in picks], axis=0)
            rows = per_tile * frames
            bias = bias_full[pl.ds(first_head, per_tile)].reshape(rows, extended)
            scores = contract(queries, key, 1, 1) * scaling + bias
            grad_probs = contract(grads, value, 1, 1)
            top = jnp.max(scores, axis=1, keepdims=True)
            shifted = jnp.exp(scores - top)
            probs = shifted * (1.0 / jnp.sum(shifted, axis=1, keepdims=True))
            probs_low = probs.astype(jnp.bfloat16)
            delta = jnp.sum(probs * grad_probs, axis=1, keepdims=True)
            grad_scores = probs * (grad_probs - delta)
            grad_low = grad_scores.astype(jnp.bfloat16)

            dkey = contract(grad_low, queries, 0, 0)
            dvalue = contract(probs_low, grads, 0, 0)
            inner = pl.ds(tile * lane_tile, lane_tile)
            for array, part in ((0, dkey), (1, dvalue)):
                low = part.astype(jnp.bfloat16)
                back_send[0, chunk, array, :, inner] = low[:frames]
                back_send[1, chunk, array, :, inner] = low[2 * frames :]
                key_sums[array, :, cols] = part[frames : 2 * frames]

            mixed = contract(probs_low, value, 1, 0)
            dquery = contract(grad_low, key, 1, 0)
            context = mixed[:frames]
            dquery_out = dquery[:frames]
            for sub in range(1, per_tile):
                here = lane_head == sub
                context = jnp.where(here, mixed[sub * frames : (sub + 1) * frames], context)
                dquery_out = jnp.where(here, dquery[sub * frames : (sub + 1) * frames], dquery_out)
            staged[0, :, cols] = jnp.where(valid, context, 0.0).astype(jnp.bfloat16)
            staged[1, :, cols] = (dquery_out * scaling).astype(jnp.bfloat16)

            for sub in range(per_tile):
                folded = grad_scores[sub * frames : (sub + 1) * frames]
                half = frames // 2
                while half >= 8:
                    folded = folded[:half] + pltpu.roll(folded[half:], extended - half, 1)
                    half //= 2
                diag_sums[pl.ds((first_head + sub) * 8, 8), :] = folded
        for side in (0, 1):
            when_side(side, lambda: back_copy(side, chunk).start())
        store(4 * chunk, staged.at[0, :, lanes(chunk)], context_hbm.at[0, :, lanes(chunk)])
        store(4 * chunk + 1, staged.at[1, :, lanes(chunk)], dquery_hbm.at[0, :, lanes(chunk)])

    folded = diag_sums[...]
    turn = lax.rem(lax.broadcasted_iota(jnp.int32, folded.shape, 0), 8)
    for bit in (1, 2, 4):
        moved = pltpu.roll(folded, extended - bit, 1)
        folded = jnp.where(lax.rem(lax.div(turn, bit), 2) == 1, moved, folded)
    table = jnp.sum(folded.reshape(heads, 8, extended), axis=1)

    def table_copy(level, base, slot_from, slot_to, device):
        return pltpu.make_async_remote_copy(
            src_ref=tables.at[base + slot_from],
            dst_ref=tables.at[base + slot_from],
            send_sem=table_send_sem.at[base + slot_to],
            recv_sem=table_recv_sem.at[base + slot_from],
            device_id=device(slot_to),
            device_id_type=MESH,
        )

    def send_tables(level, base, table):
        mine, others, device, total = groups[level]
        tables[base + mine, pl.ds(0, heads), :] = table
        for slot in others:
            table_copy(level, base, mine, slot, device).start()

    def sum_tables(level, base):
        mine, others, device, total = groups[level]
        for slot in others:
            table_copy(level, base, slot, slot, device).wait_recv()
        whole = tables[base, pl.ds(0, heads), :]
        for slot in range(1, total):
            whole = whole + tables[base + slot, pl.ds(0, heads), :]
        return whole

    bases = []
    used = 0
    for mine, others, device, total in groups:
        bases.append(used)
        used += total

    def finish_keys():
        for chunk in range(chunks):
            for side in (0, 1):
                when_side(1 - side, lambda: back_copy(side, chunk).wait_recv())
            for array in (0, 1):
                cols = lanes(chunk)
                whole = (
                    key_sums[array, :, cols]
                    + back_recv[0, chunk, array].astype(jnp.float32)
                    + back_recv[1, chunk, array].astype(jnp.float32)
                )
                if array == 0:
                    whole = whole * scaling
                staged[2 + array, :, cols] = whole.astype(jnp.bfloat16)
                store(
                    4 * chunk + 2 + array,
                    staged.at[2 + array, :, cols],
                    (dkey_hbm, dvalue_hbm)[array].at[0, :, cols],
                )

    send_tables(0, bases[0], table)
    finish_keys()
    table = sum_tables(0, bases[0])
    for level in range(1, len(groups)):
        send_tables(level, bases[level], table)
        table = sum_tables(level, bases[level])
    dbias_ref[...] = table[:, :span]

    for level, (mine, others, device, total) in enumerate(groups):
        for slot in others:
            table_copy(level, bases[level], mine, slot, device).wait_send()
    for chunk in range(chunks):
        for side in (0, 1):
            when_side(side, lambda: back_copy(side, chunk).wait_send())
            for array in (0, 1):
                when_side(1 - side, lambda: rim_copy(side, array, chunk).wait_send())
    for copy in stores:
        copy.wait()


def on_device(n_dp, n_tm, query_proj, key_proj, value_proj, cotangent, lengths, rel_bias):
    frames, width = query_proj.shape[1:]
    heads, span = rel_bias.shape
    head_size = width // heads
    extended = 3 * frames
    chunk_lanes = 2 * lane_tile
    chunks = width // chunk_lanes
    slots = sum(size * (n_dp if with_dp else 1) for _, size, with_dp in sum_stages(n_dp, n_tm))
    plan = (n_dp, n_tm, heads, frames, head_size, span, chunks, chunk_lanes)
    block = jax.ShapeDtypeStruct((1, frames, width), jnp.bfloat16)
    low = jnp.bfloat16
    padded_heads = -(-heads // 8) * 8
    hbm = pl.BlockSpec(memory_space=pl.ANY)
    vmem = pl.BlockSpec(memory_space=pltpu.VMEM)
    return pl.pallas_call(
        functools.partial(kernel, plan),
        out_shape=(block, block, block, block, jax.ShapeDtypeStruct((heads, span), jnp.float32)),
        in_specs=[pl.BlockSpec(memory_space=pltpu.SMEM), vmem, hbm, hbm, hbm, hbm],
        out_specs=(hbm, hbm, hbm, hbm, vmem),
        scratch_shapes=[
            pltpu.VMEM((2, extended, width), low),
            pltpu.VMEM((2, frames, width), low),
            pltpu.VMEM((padded_heads, extended), jnp.float32),
            pltpu.VMEM((heads, frames, extended), jnp.float32),
            pltpu.VMEM((4, frames, width), low),
            pltpu.VMEM((2, frames, width), jnp.float32),
            pltpu.VMEM((2, chunks, 2, frames, chunk_lanes), low),
            pltpu.VMEM((2, chunks, 2, frames, chunk_lanes), low),
            pltpu.VMEM((heads * 8, extended), jnp.float32),
            pltpu.VMEM((slots, padded_heads, extended), jnp.float32),
            pltpu.SemaphoreType.DMA((4,)),
            pltpu.SemaphoreType.DMA((4 * chunks,)),
            pltpu.SemaphoreType.DMA((2, 2, chunks)),
            pltpu.SemaphoreType.DMA((2, 2, chunks)),
            pltpu.SemaphoreType.DMA((2, chunks)),
            pltpu.SemaphoreType.DMA((2, chunks)),
            pltpu.SemaphoreType.DMA((slots,)),
            pltpu.SemaphoreType.DMA((slots,)),
        ],
        compiler_params=pltpu.CompilerParams(
            collective_id=0, has_side_effects=True, vmem_limit_bytes=40 * 1024 * 1024
        ),
    )(lengths, rel_bias, query_proj, key_proj, value_proj, cotangent)


def solution(mesh):
    rows = P("dp", "tm", None)
    return jax.shard_map(
        functools.partial(on_device, mesh.shape["dp"], mesh.shape["tm"]),
        mesh=mesh,
        in_specs=(rows, rows, rows, rows, P("dp"), P()),
        out_specs=(rows, rows, rows, rows, P()),
        check_vma=False,
    )
```

time: 118 us -> 41.9 us (0.36)
  blocking collectives: 42.9 us -> 0 us
  Pallas kernels: 0 us -> 32.6 us
  local copies, waits for them, and re-layouts: 33.6 us -> 7.75 us
  matrix products: 16.5 us -> 0 us
  other arithmetic: 11.4 us -> 0 us
  starting transfers between devices: 10.9 us -> 0 us
    psum x1 -> x0, blocking collectives: 42.9 us -> none  [on_device(): grad_bias = lax.psum(grad_table, ('dp', 'tm'))]
    pallas_call x0 -> x1, Pallas kernels: none -> 32.6 us  [on_device(): pl.pallas_call(functools.partial(kernel, plan), out_shape=(block, block,...]
    dot_general x21 -> x0, matrix products: 16.5 us -> none  [the longest x3 4.69 us: key_side(): jnp.einsum('hkq,hqd->hkd', grad_low, query_rows, preferred_element_type=j...]
    reshape x15 -> x0, local copies, waits for them, and re-layouts: 15.3 us -> none  [the longest x6 6.24 us: band_matrix(): padded.reshape(num_heads, height * (breadth + 1))[:, :height * breadth]]
    ppermute x4 -> x0, starting transfers between devices: 10.9 us -> none  [the longest x2 8.32 us: padded_2(): lax.ppermute(tail, axis, [(i, (i + 1) % count) for i in range(ends)])]
    concatenate x6 -> x0, other arithmetic: 4.15 us -> none  [the longest x1 1.56 us: padded_2(): jnp.concatenate([lax.ppermute(tail, axis, [(i, (i + 1) % count) for i in...]
    unnamed x69 -> x15, local copies, waits for them, and re-layouts: 11.7 us -> 7.75 us
    mul x3 -> x0, local copies, waits for them, and re-layouts: 3.46 us -> none  [query_side(): grad_scores = attn_probs * (grad_probs - row_delta[..., None])]
  transfers between devices with their start and end apart: 4 -> 0, of which waited for: 0 -> 0; matrix products, arithmetic and copies ran while one was open for 30% -> 0% of each run, Pallas kernels for 0% -> 0%
where the time goes in v1:
time: 41.9 us; the launch traced here: 41.7 us
  Pallas kernels  32.6 us (78%)
  local copies, waits for them, and re-layouts  7.75 us (18%)
  between operations  1.3 us (3%)
    pallas_call x1, Pallas kernels, on_device(): pl.pallas_call(functools.partial(kernel, plan), out_shape=(block, block,...  32.6 us
    unnamed x15, local copies, waits for them, and re-layouts  7.75 us

profile of v1, /device:TPU:0, one launch (start us, length us, event | category | flops | bytes accessed | tf_op | source)
XLA Modules:
  0.0 41.7 jit_solution(6958670705622743225)
XLA Ops:
  1.3 0.0 copy-start
  1.3 0.9 %copy-done = bf16[1,128,768]{2,1,0:T(8,128)(2,1)S(1)} copy-done((bf16[1,128,768]{2,1,0:T(8,128)(2,1)S(1)}, bf16[1,128,768]{2,1,0:T(8,128)(2,1)}, u32[]{:S(2)}) %copy-start) | copy-done | bytes 196632
  2.2 0.0 copy-start.1
  2.2 0.9 %copy-done.1 = bf16[1,128,768]{2,1,0:T(8,128)(2,1)S(1)} copy-done((bf16[1,128,768]{2,1,0:T(8,128)(2,1)S(1)}, bf16[1,128,768]{2,1,0:T(8,128)(2,1)}, u32[]{:S(2)}) %copy-start.1) | copy-done | bytes 196632
  3.1 0.0 copy-start.2
  3.1 0.9 %copy-done.2 = bf16[1,128,768]{2,1,0:T(8,128)(2,1)S(1)} copy-done((bf16[1,128,768]{2,1,0:T(8,128)(2,1)S(1)}, bf16[1,128,768]{2,1,0:T(8,128)(2,1)}, u32[]{:S(2)}) %copy-start.2) | copy-done | bytes 196632
  4.1 0.0 copy-start.3
  4.1 0.9 %copy-done.3 = bf16[1,128,768]{2,1,0:T(8,128)(2,1)S(1)} copy-done((bf16[1,128,768]{2,1,0:T(8,128)(2,1)S(1)}, bf16[1,128,768]{2,1,0:T(8,128)(2,1)}, u32[]{:S(2)}) %copy-start.3) | copy-done | bytes 196632
  5.0 0.0 copy-start.4
  5.0 0.7 %copy-done.4 = f32[12,257]{1,0:T(8,128)S(1)} copy-done((f32[12,257]{1,0:T(8,128)S(1)}, f32[12,257]{1,0:T(8,128)}, u32[]{:S(2)}) %copy-start.4) | copy-done | bytes 12360
  5.7 32.6 %shard_map.101 = (bf16[1,128,768]{2,1,0:T(8,128)(2,1)S(1)}, bf16[1,128,768]{2,1,0:T(8,128)(2,1)S(1)}, bf16[1,128,768]{2,1,0:T(8,128)(2,1)S(1)}, bf16[1,128,768]{2,1,0:T(8,128)(2,1)S(1)}, f32[12,257]{1,0:T(8,128)S(1)}) custom-call(s32[1]{0:T(128)S(6)} %copy.16.length_ref, f32[12,257]{1,0:T(8,128)S(1)} %copy-done.4, bf16[1,128,768]{2,1,0:T(8,128)(2,1)S(1)} %copy-done, ...), custom_call_target="tpu_custom_call" | custom-call | tf_op jit(solution)/shard_map/pallas_call | solution.py:342
  38.3 0.7 %copy.17 = bf16[1,128,768]{2,1,0:T(8,128)(2,1)} copy(bf16[1,128,768]{2,1,0:T(8,128)(2,1)S(1)} %get-tuple-element.10) | data formatting | bytes 393216
  39.0 0.7 %copy.18 = bf16[1,128,768]{2,1,0:T(8,128)(2,1)} copy(bf16[1,128,768]{2,1,0:T(8,128)(2,1)S(1)} %get-tuple-element.11) | data formatting | bytes 393216
  39.7 0.7 %copy.19 = bf16[1,128,768]{2,1,0:T(8,128)(2,1)} copy(bf16[1,128,768]{2,1,0:T(8,128)(2,1)S(1)} %get-tuple-element.12) | data formatting | bytes 393216
  40.4 0.7 %copy.20 = bf16[1,128,768]{2,1,0:T(8,128)(2,1)} copy(bf16[1,128,768]{2,1,0:T(8,128)(2,1)S(1)} %get-tuple-element.13) | data formatting | bytes 393216
  41.1 0.6 %copy.21 = f32[12,257]{1,0:T(8,128)} copy(f32[12,257]{1,0:T(8,128)S(1)} %get-tuple-element.14) | data formatting | bytes 24672
Async XLA Ops:
  1.3 0.9 %copy-start = (bf16[1,128,768]{2,1,0:T(8,128)(2,1)S(1)}, bf16[1,128,768]{2,1,0:T(8,128)(2,1)}, u32[]{:S(2)}) copy-start(bf16[1,128,768]{2,1,0:T(8,128)(2,1)} %query_hbm.1) | copy-start | bytes 589828
  2.2 0.9 %copy-start.1 = (bf16[1,128,768]{2,1,0:T(8,128)(2,1)S(1)}, bf16[1,128,768]{2,1,0:T(8,128)(2,1)}, u32[]{:S(2)}) copy-start(bf16[1,128,768]{2,1,0:T(8,128)(2,1)} %key_hbm.1) | copy-start | bytes 589828
  3.1 0.9 %copy-start.2 = (bf16[1,128,768]{2,1,0:T(8,128)(2,1)S(1)}, bf16[1,128,768]{2,1,0:T(8,128)(2,1)}, u32[]{:S(2)}) copy-start(bf16[1,128,768]{2,1,0:T(8,128)(2,1)} %value_hbm.1) | copy-start | bytes 589828
  4.1 0.9 %copy-start.3 = (bf16[1,128,768]{2,1,0:T(8,128)(2,1)S(1)}, bf16[1,128,768]{2,1,0:T(8,128)(2,1)}, u32[]{:S(2)}) copy-start(bf16[1,128,768]{2,1,0:T(8,128)(2,1)} %grad_hbm.1) | copy-start | bytes 589828
  5.0 0.7 %copy-start.4 = (f32[12,257]{1,0:T(8,128)S(1)}, f32[12,257]{1,0:T(8,128)}, u32[]{:S(2)}) copy-start(f32[12,257]{1,0:T(8,128)} %bias_ref.1) | copy-start | bytes 37012

commit v2 on v1

--- a/solution.py
+++ b/solution.py
@@ -34,7 +34,7 @@
 def kernel(
     plan,
     length_ref,
-    bias_ref,
+    bias_hbm,
     query_hbm,
     key_hbm,
     value_hbm,
@@ -43,9 +43,10 @@
     dquery_hbm,
     dkey_hbm,
     dvalue_hbm,
-    dbias_ref,
+    dbias_hbm,
     ext,
     own,
+    bias_ref,
     bias_rows,
     bias_full,
     staged,
@@ -81,6 +82,8 @@
         pltpu.make_async_copy(key_hbm.at[0], ext.at[0, pl.ds(frames, frames)], load_sem.at[2]),
         pltpu.make_async_copy(value_hbm.at[0], ext.at[1, pl.ds(frames, frames)], load_sem.at[3]),
     ]
+    bias_load = pltpu.make_async_copy(bias_hbm, bias_ref, load_sem.at[4])
+    bias_load.start()
     for copy in loads:
         copy.start()
 
@@ -133,12 +136,12 @@
             device_id_type=MESH,
         )
 
-    def back_copy(side, chunk):
+    def back_copy(side, tile):
         return pltpu.make_async_remote_copy(
-            src_ref=back_send.at[side, chunk],
-            dst_ref=back_recv.at[side, chunk],
-            send_sem=back_send_sem.at[side, chunk],
-            recv_sem=back_recv_sem.at[side, chunk],
+            src_ref=back_send.at[side, tile],
+            dst_ref=back_recv.at[side, tile],
+            send_sem=back_send_sem.at[side, tile],
+            recv_sem=back_recv_sem.at[side, tile],
             device_id=(dp, tm - 1 + 2 * side),
             device_id_type=MESH,
         )
@@ -161,21 +164,42 @@
     first = tm * frames
     row = lax.broadcasted_iota(jnp.int32, (frames, extended), 0)
     column = lax.broadcasted_iota(jnp.int32, (frames, extended), 1)
-    offset = column - row
-    key_pos = first - frames + column
-    allowed = (offset >= 0) & (offset < span) & (key_pos >= 0) & (key_pos < length)
+    place = column - row
+    key_pos = first + frames - lax.div(column, frames) * frames + row
+    allowed = (place >= 0) & (place < span) & (key_pos >= 0) & (key_pos < length)
+    flip_row = lax.broadcasted_iota(jnp.int32, (extended, extended), 0)
+    flip_column = lax.broadcasted_iota(jnp.int32, (extended, extended), 1)
+    mirror = jnp.where(flip_row + flip_column == span - 1, 1.0, 0.0)
+
+    def mirrored(table):
+        return lax.dot_general(
+            table,
+            mirror,
+            (((1,), (0,)), ((), ())),
+            precision=lax.Precision.HIGHEST,
+            preferred_element_type=jnp.float32,
+        )
+
+    per_tile = lane_tile // head_size
+    bias_load.wait()
     bias_rows[...] = jnp.zeros_like(bias_rows)
     bias_rows[pl.ds(0, heads), pl.ds(0, span)] = bias_ref[...]
+    bias_rows[...] = mirrored(bias_rows[...])
     for head in range(heads):
         spread = jnp.broadcast_to(bias_rows[pl.ds(head, 1), :], (frames, extended))
         rolled = pltpu.roll(spread, 0, 1, stride=1, stride_axis=0)
-        bias_full[head] = jnp.where(allowed, rolled, masked_score)
+        masked = jnp.where(allowed, rolled, masked_score)
+        for part in range(3):
+            bias_full[
+                head // per_tile,
+                pl.ds(part * frames, frames),
+                pl.ds((head % per_tile) * frames, frames),
+            ] = masked[:, (2 - part) * frames : (3 - part) * frames]
 
     query_row = lax.broadcasted_iota(jnp.int32, (frames, lane_tile), 0)
     lane = lax.broadcasted_iota(jnp.int32, (frames, lane_tile), 1)
     valid = first + query_row < length
     valid_low = jnp.where(valid, 1.0, 0.0).astype(jnp.bfloat16)
-    per_tile = lane_tile // head_size
     lane_head = lax.div(lane, head_size)
     picks = [jnp.where(lane_head == sub, 1.0, 0.0).astype(jnp.bfloat16) for sub in range(per_tile)]
 
@@ -189,63 +213,81 @@
         copy.start()
         stores.append(copy)
 
+    def softmax_part(tile):
+        cols = pl.ds(tile * lane_tile, lane_tile)
+        query = own[0, :, cols]
+        grad = own[1, :, cols] * valid_low
+        key = ext[0, :, cols]
+        value = ext[1, :, cols]
+        queries = jnp.concatenate([query * pick for pick in picks], axis=0)
+        grads = jnp.concatenate([grad * pick for pick in picks], axis=0)
+        scores = contract(key, queries, 1, 1) * scaling + bias_full[tile]
+        grad_probs = contract(value, grads, 1, 1)
+        top = jnp.max(scores, axis=0, keepdims=True)
+        shifted = jnp.exp(scores - top)
+        probs = shifted * (1.0 / jnp.sum(shifted, axis=0, keepdims=True))
+        probs_low = probs.astype(jnp.bfloat16)
+        delta = jnp.sum(probs * grad_probs, axis=0, keepdims=True)
+        grad_scores = probs * (grad_probs - delta)
+        grad_low = grad_scores.astype(jnp.bfloat16)
+        for sub in range(per_tile):
+            mine = grad_scores[:, sub * frames : (sub + 1) * frames]
+            folded = jnp.concatenate(
+                [mine[part * frames : (part + 1) * frames] for part in (2, 1, 0)], axis=1
+            )
+            half = frames // 2
+            while half >= 8:
+                folded = folded[:half] + pltpu.roll(folded[half:], extended - half, 1)
+                half //= 2
+            diag_sums[pl.ds((tile * per_tile + sub) * 8, 8), :] = folded
+        return queries, grads, probs_low, grad_low
+
+    def product_part(tile, held):
+        queries, grads, probs_low, grad_low = held
+        cols = pl.ds(tile * lane_tile, lane_tile)
+        key = ext[0, :, cols]
+        value = ext[1, :, cols]
+        for array, part in (
+            (0, contract(grad_low, queries, 1, 0)),
+            (1, contract(probs_low, grads, 1, 0)),
+        ):
+            low = part.astype(jnp.bfloat16)
+            back_send[0, tile, array] = low[:frames]
+            back_send[1, tile, array] = low[2 * frames :]
+            key_sums[array, :, cols] = part[frames : 2 * frames]
+
+        def own_heads(turned):
+            parts = [
+                turned[sub * head_size : (sub + 1) * head_size, sub * frames : (sub + 1) * frames]
+                for sub in range(per_tile)
+            ]
+            return jnp.concatenate(parts, axis=0).T
+
+        context = own_heads(contract(value, probs_low, 0, 0))
+        dquery = own_heads(contract(key, grad_low, 0, 0))
+        staged[0, :, cols] = jnp.where(valid, context, 0.0).astype(jnp.bfloat16)
+        staged[1, :, cols] = (dquery * scaling).astype(jnp.bfloat16)
+
+    def give_back(tile):
+        for side in (0, 1):
+            when_side(side, lambda: back_copy(side, tile).start())
+
+    per_chunk = chunk_lanes // lane_tile
+    tiles = chunks * per_chunk
+    held = None
     for chunk in range(chunks):
         for array in (0, 1):
             for side in (0, 1):
                 when_side(side, lambda: rim_copy(side, array, chunk).wait_recv())
-        for tile in range(chunk_lanes // lane_tile):
-            start = chunk * chunk_lanes + tile * lane_tile
-            cols = pl.ds(start, lane_tile)
-            first_head = start // head_size
-            query = own[0, :, cols]
-            grad = own[1, :, cols] * valid_low
-            key = ext[0, :, cols]
-            value = ext[1, :, cols]
-            queries = jnp.concatenate([query * pick for pick in picks], axis=0)
-            grads = jnp.concatenate([grad * pick for pick in picks], axis=0)
-            rows = per_tile * frames
-            bias = bias_full[pl.ds(first_head, per_tile)].reshape(rows, extended)
-            scores = contract(queries, key, 1, 1) * scaling + bias
-            grad_probs = contract(grads, value, 1, 1)
-            top = jnp.max(scores, axis=1, keepdims=True)
-            shifted = jnp.exp(scores - top)
-            probs = shifted * (1.0 / jnp.sum(shifted, axis=1, keepdims=True))
-            probs_low = probs.astype(jnp.bfloat16)
-            delta = jnp.sum(probs * grad_probs, axis=1, keepdims=True)
-            grad_scores = probs * (grad_probs - delta)
-            grad_low = grad_scores.astype(jnp.bfloat16)
-
-            dkey = contract(grad_low, queries, 0, 0)
-            dvalue = contract(probs_low, grads, 0, 0)
-            inner = pl.ds(tile * lane_tile, lane_tile)
-            for array, part in ((0, dkey), (1, dvalue)):
-                low = part.astype(jnp.bfloat16)
-                back_send[0, chunk, array, :, inner] = low[:frames]
-                back_send[1, chunk, array, :, inner] = low[2 * frames :]
-                key_sums[array, :, cols] = part[frames : 2 * frames]
-
-            mixed = contract(probs_low, value, 1, 0)
-            dquery = contract(grad_low, key, 1, 0)
-            context = mixed[:frames]
-            dquery_out = dquery[:frames]
-            for sub in range(1, per_tile):
-                here = lane_head == sub
-                context = jnp.where(here, mixed[sub * frames : (sub + 1) * frames], context)
-                dquery_out = jnp.where(here, dquery[sub * frames : (sub + 1) * frames], dquery_out)
-            staged[0, :, cols] = jnp.where(valid, context, 0.0).astype(jnp.bfloat16)
-            staged[1, :, cols] = (dquery_out * scaling).astype(jnp.bfloat16)
-
-            for sub in range(per_tile):
-                folded = grad_scores[sub * frames : (sub + 1) * frames]
-                half = frames // 2
-                while half >= 8:
-                    folded = folded[:half] + pltpu.roll(folded[half:], extended - half, 1)
-                    half //= 2
-                diag_sums[pl.ds((first_head + sub) * 8, 8), :] = folded
-        for side in (0, 1):
-            when_side(side, lambda: back_copy(side, chunk).start())
-        store(4 * chunk, staged.at[0, :, lanes(chunk)], context_hbm.at[0, :, lanes(chunk)])
-        store(4 * chunk + 1, staged.at[1, :, lanes(chunk)], dquery_hbm.at[0, :, lanes(chunk)])
+        done = []
+        for tile in range(chunk * per_chunk, (chunk + 1) * per_chunk):
+            fresh = softmax_part(tile)
+            if held is not None:
+                product_part(tile - 1, held)
+                done.append(tile - 1)
+            held = fresh
+        for tile in done:
+            give_back(tile)
 
     folded = diag_sums[...]
     turn = lax.rem(lax.broadcasted_iota(jnp.int32, folded.shape, 0), 8)
@@ -286,39 +328,46 @@
         used += total
 
     def finish_keys():
-        for chunk in range(chunks):
+        for tile in range(tiles):
             for side in (0, 1):
-                when_side(1 - side, lambda: back_copy(side, chunk).wait_recv())
+                when_side(1 - side, lambda: back_copy(side, tile).wait_recv())
             for array in (0, 1):
-                cols = lanes(chunk)
+                cols = pl.ds(tile * lane_tile, lane_tile)
                 whole = (
                     key_sums[array, :, cols]
-                    + back_recv[0, chunk, array].astype(jnp.float32)
-                    + back_recv[1, chunk, array].astype(jnp.float32)
+                    + back_recv[0, tile, array].astype(jnp.float32)
+                    + back_recv[1, tile, array].astype(jnp.float32)
                 )
                 if array == 0:
                     whole = whole * scaling
                 staged[2 + array, :, cols] = whole.astype(jnp.bfloat16)
-                store(
-                    4 * chunk + 2 + array,
-                    staged.at[2 + array, :, cols],
-                    (dkey_hbm, dvalue_hbm)[array].at[0, :, cols],
-                )
+        store(2, staged.at[2], dkey_hbm.at[0])
+        store(3, staged.at[3], dvalue_hbm.at[0])
 
     send_tables(0, bases[0], table)
-    finish_keys()
+    product_part(tiles - 1, held)
+    give_back(tiles - 1)
+    store(0, staged.at[0], context_hbm.at[0])
+    store(1, staged.at[1], dquery_hbm.at[0])
     table = sum_tables(0, bases[0])
     for level in range(1, len(groups)):
         send_tables(level, bases[level], table)
+        if level == 1:
+            finish_keys()
         table = sum_tables(level, bases[level])
-    dbias_ref[...] = table[:, :span]
+    if len(groups) == 1:
+        finish_keys()
+    bias_rows[pl.ds(0, heads), :] = table
+    bias_ref[...] = mirrored(bias_rows[...])[:heads, :span]
+    store(4, bias_ref, dbias_hbm)
 
     for level, (mine, others, device, total) in enumerate(groups):
         for slot in others:
             table_copy(level, bases[level], mine, slot, device).wait_send()
-    for chunk in range(chunks):
-        for side in (0, 1):
-            when_side(side, lambda: back_copy(side, chunk).wait_send())
+    for side in (0, 1):
+        for tile in range(tiles):
+            when_side(side, lambda: back_copy(side, tile).wait_send())
+        for chunk in range(chunks):
             for array in (0, 1):
                 when_side(1 - side, lambda: rim_copy(side, array, chunk).wait_send())
     for copy in stores:
@@ -337,37 +386,60 @@
     block = jax.ShapeDtypeStruct((1, frames, width), jnp.bfloat16)
     low = jnp.bfloat16
     padded_heads = -(-heads // 8) * 8
-    hbm = pl.BlockSpec(memory_space=pl.ANY)
-    vmem = pl.BlockSpec(memory_space=pltpu.VMEM)
-    return pl.pallas_call(
+    anywhere = pl.BlockSpec(memory_space=pl.ANY)
+    hbm = pl.BlockSpec(memory_space=pltpu.HBM)
+    tiles = width // lane_tile
+    shapes = (block, block, block, block, jax.ShapeDtypeStruct((heads, span), jnp.float32))
+    results = pl.pallas_call(
         functools.partial(kernel, plan),
-        out_shape=(block, block, block, block, jax.ShapeDtypeStruct((heads, span), jnp.float32)),
-        in_specs=[pl.BlockSpec(memory_space=pltpu.SMEM), vmem, hbm, hbm, hbm, hbm],
-        out_specs=(hbm, hbm, hbm, hbm, vmem),
+        out_shape=shapes,
+        in_specs=[pl.BlockSpec(memory_space=pltpu.SMEM)] + [hbm] * 5,
+        out_specs=(anywhere,) * 5,
         scratch_shapes=[
             pltpu.VMEM((2, extended, width), low),
             pltpu.VMEM((2, frames, width), low),
+            pltpu.VMEM((heads, span), jnp.float32),
             pltpu.VMEM((padded_heads, extended), jnp.float32),
-            pltpu.VMEM((heads, frames, extended), jnp.float32),
+            pltpu.VMEM((tiles, extended, lane_tile // head_size * frames), jnp.float32),
             pltpu.VMEM((4, frames, width), low),
             pltpu.VMEM((2, frames, width), jnp.float32),
-            pltpu.VMEM((2, chunks, 2, frames, chunk_lanes), low),
-            pltpu.VMEM((2, chunks, 2, frames, chunk_lanes), low),
+            pltpu.VMEM((2, tiles, 2, frames, lane_tile), low),
+            pltpu.VMEM((2, tiles, 2, frames, lane_tile), low),
             pltpu.VMEM((heads * 8, extended), jnp.float32),
             pltpu.VMEM((slots, padded_heads, extended), jnp.float32),
-            pltpu.SemaphoreType.DMA((4,)),
-            pltpu.SemaphoreType.DMA((4 * chunks,)),
+            pltpu.SemaphoreType.DMA((5,)),
+            pltpu.SemaphoreType.DMA((5,)),
             pltpu.SemaphoreType.DMA((2, 2, chunks)),
             pltpu.SemaphoreType.DMA((2, 2, chunks)),
-            pltpu.SemaphoreType.DMA((2, chunks)),
-            pltpu.SemaphoreType.DMA((2, chunks)),
+            pltpu.SemaphoreType.DMA((2, tiles)),
+            pltpu.SemaphoreType.DMA((2, tiles)),
             pltpu.SemaphoreType.DMA((slots,)),
             pltpu.SemaphoreType.DMA((slots,)),
         ],
         compiler_params=pltpu.CompilerParams(
-            collective_id=0, has_side_effects=True, vmem_limit_bytes=40 * 1024 * 1024
+            collective_id=0, has_side_effects=True, vmem_limit_bytes=60 * 1024 * 1024
         ),
     )(lengths, rel_bias, query_proj, key_proj, value_proj, cotangent)
+    return pl.pallas_call(
+        hand_over,
+        out_shape=shapes,
+        in_specs=[anywhere] * 5,
+        out_specs=(hbm,) * 5,
+        scratch_shapes=[pltpu.SemaphoreType.DMA((5,))],
+        compiler_params=pltpu.CompilerParams(vmem_limit_bytes=60 * 1024 * 1024),
+    )(*results)
+
+
+def hand_over(*refs):
+    sources, targets, sems = refs[:5], refs[5:10], refs[10]
+    copies = [
+        pltpu.make_async_copy(source, target, sems.at[index])
+        for index, (source, target) in enumerate(zip(sources, targets))
+    ]
+    for copy in copies:
+        copy.start()
+    for copy in copies:
+        copy.wait()
 
 
 def solution(mesh):

time: 41.9 us -> 59.3 us (1.42)
  Pallas kernels: 32.6 us -> 57.8 us
  local copies, waits for them, and re-layouts: 7.75 us -> 0 us
    pallas_call x1 -> x2, Pallas kernels: 32.6 us -> 57.8 us  [the longest x1 32.1 us: on_device(): pl.pallas_call(functools.partial(kernel, plan), out_shape=shapes, in_spec...]
    unnamed x15 -> x0, local copies, waits for them, and re-layouts: 7.75 us -> none
where the time goes in v2:
time: 59.3 us; the launch traced here: 59.1 us
  Pallas kernels  57.8 us (97%)
  between operations  1.29 us (2%)
    pallas_call x1, Pallas kernels, on_device(): pl.pallas_call(functools.partial(kernel, plan), out_shape=shapes, in_spec...  32.1 us
    pallas_call x1, Pallas kernels, on_device(): pl.pallas_call(hand_over, out_shape=shapes, in_specs=[anywhere] * 5, out_...  25.7 us

profile of v2, /device:TPU:0, one launch (start us, length us, event | category | flops | bytes accessed | tf_op | source)
XLA Modules:
  0.0 59.1 jit_solution(11545329394913729896)
XLA Ops:
  1.3 32.1 %shard_map.101 = (bf16[1,128,768]{2,1,0:T(8,128)(2,1)}, bf16[1,128,768]{2,1,0:T(8,128)(2,1)}, bf16[1,128,768]{2,1,0:T(8,128)(2,1)}, bf16[1,128,768]{2,1,0:T(8,128)(2,1)}, f32[12,257]{1,0:T(8,128)}) custom-call(s32[1]{0:T(128)S(6)} %copy.11.length_ref, f32[12,257]{1,0:T(8,128)} %bias_hbm.1, bf16[1,128,768]{2,1,0:T(8,128)(2,1)} %query_hbm.1, ...), custom_call_target="tpu_custom_call" | custom-call | tf_op jit(solution)/shard_map/pallas_call | solution.py:393
  33.4 25.7 %shard_map.102 = (bf16[1,128,768]{2,1,0:T(8,128)(2,1)}, bf16[1,128,768]{2,1,0:T(8,128)(2,1)}, bf16[1,128,768]{2,1,0:T(8,128)(2,1)}, bf16[1,128,768]{2,1,0:T(8,128)(2,1)}, f32[12,257]{1,0:T(8,128)}) custom-call(bf16[1,128,768]{2,1,0:T(8,128)(2,1)} %get-tuple-element.10.refs_0_, bf16[1,128,768]{2,1,0:T(8,128)(2,1)} %get-tuple-element.11.refs_1_, ...), custom_call_target="tpu_custom_call" | custom-call | tf_op jit(solution)/shard_map/pallas_call | solution.py:423

commit v3 on v2

--- a/solution.py
+++ b/solution.py
@@ -165,7 +165,8 @@
     row = lax.broadcasted_iota(jnp.int32, (frames, extended), 0)
     column = lax.broadcasted_iota(jnp.int32, (frames, extended), 1)
     place = column - row
-    key_pos = first + frames - lax.div(column, frames) * frames + row
+    block = jnp.where(column < frames, 1, jnp.where(column < 2 * frames, 0, -1))
+    key_pos = first + block * frames + row
     allowed = (place >= 0) & (place < span) & (key_pos >= 0) & (key_pos < length)
     flip_row = lax.broadcasted_iota(jnp.int32, (extended, extended), 0)
     flip_column = lax.broadcasted_iota(jnp.int32, (extended, extended), 1)
@@ -185,9 +186,15 @@
     bias_rows[...] = jnp.zeros_like(bias_rows)
     bias_rows[pl.ds(0, heads), pl.ds(0, span)] = bias_ref[...]
     bias_rows[...] = mirrored(bias_rows[...])
+    spread = jnp.broadcast_to(bias_rows[pl.ds(0, heads), :][:, None, :], (heads, 8, extended))
+    spread = spread.reshape(heads * 8, extended)
+    turn = lax.broadcasted_iota(jnp.int32, spread.shape, 0) & 7
+    for bit in (1, 2, 4):
+        spread = jnp.where((turn & bit) != 0, pltpu.roll(spread, bit, 1), spread)
     for head in range(heads):
-        spread = jnp.broadcast_to(bias_rows[pl.ds(head, 1), :], (frames, extended))
-        rolled = pltpu.roll(spread, 0, 1, stride=1, stride_axis=0)
+        rolled = spread[head * 8 : (head + 1) * 8]
+        while rolled.shape[0] < frames:
+            rolled = jnp.concatenate([rolled, pltpu.roll(rolled, rolled.shape[0], 1)], axis=0)
         masked = jnp.where(allowed, rolled, masked_score)
         for part in range(3):
             bias_full[
@@ -200,8 +207,12 @@
     lane = lax.broadcasted_iota(jnp.int32, (frames, lane_tile), 1)
     valid = first + query_row < length
     valid_low = jnp.where(valid, 1.0, 0.0).astype(jnp.bfloat16)
-    lane_head = lax.div(lane, head_size)
-    picks = [jnp.where(lane_head == sub, 1.0, 0.0).astype(jnp.bfloat16) for sub in range(per_tile)]
+    picks = [
+        jnp.where((lane >= sub * head_size) & (lane < (sub + 1) * head_size), 1.0, 0.0).astype(
+            jnp.bfloat16
+        )
+        for sub in range(per_tile)
+    ]
 
     for copy in loads:
         copy.wait()
@@ -290,10 +301,9 @@
             give_back(tile)
 
     folded = diag_sums[...]
-    turn = lax.rem(lax.broadcasted_iota(jnp.int32, folded.shape, 0), 8)
     for bit in (1, 2, 4):
         moved = pltpu.roll(folded, extended - bit, 1)
-        folded = jnp.where(lax.rem(lax.div(turn, bit), 2) == 1, moved, folded)
+        folded = jnp.where((turn & bit) != 0, moved, folded)
     table = jnp.sum(folded.reshape(heads, 8, extended), axis=1)
 
     def table_copy(level, base, slot_from, slot_to, device):
@@ -390,9 +400,10 @@
     hbm = pl.BlockSpec(memory_space=pltpu.HBM)
     tiles = width // lane_tile
     shapes = (block, block, block, block, jax.ShapeDtypeStruct((heads, span), jnp.float32))
+    held_shapes = tuple(pltpu.VMEM(item.shape, item.dtype) for item in shapes)
     results = pl.pallas_call(
         functools.partial(kernel, plan),
-        out_shape=shapes,
+        out_shape=held_shapes,
         in_specs=[pl.BlockSpec(memory_space=pltpu.SMEM)] + [hbm] * 5,
         out_specs=(anywhere,) * 5,
         scratch_shapes=[
@@ -426,7 +437,7 @@
         in_specs=[anywhere] * 5,
         out_specs=(hbm,) * 5,
         scratch_shapes=[pltpu.SemaphoreType.DMA((5,))],
-        compiler_params=pltpu.CompilerParams(vmem_limit_bytes=60 * 1024 * 1024),
+        compiler_params=pltpu.CompilerParams(vmem_limit_bytes=8 * 1024 * 1024),
     )(*results)
 
 

time: 59.3 us -> 33.9 us (0.57)
  Pallas kernels: 57.8 us -> 32.5 us
    pallas_call x1, Pallas kernels: 25.7 us -> 0.92 us  [on_device(): pl.pallas_call(hand_over, out_shape=shapes, in_specs=[anywhere] * 5, out_...]
where the time goes in v3:
time: 33.9 us; the launch traced here: 33.8 us
  Pallas kernels  32.5 us (96%)
  between operations  1.29 us (4%)
    pallas_call x1, Pallas kernels, on_device(): pl.pallas_call(functools.partial(kernel, plan), out_shape=held_shapes, in...  31.5 us
    pallas_call x1, Pallas kernels, on_device(): pl.pallas_call(hand_over, out_shape=shapes, in_specs=[anywhere] * 5, out_...  0.92 us

profile of v3, /device:TPU:0, one launch (start us, length us, event | category | flops | bytes accessed | tf_op | source)
XLA Modules:
  0.0 33.8 jit_solution(12929946167214094009)
XLA Ops:
  1.3 31.5 %shard_map.101 = (bf16[1,128,768]{2,1,0:T(8,128)(2,1)S(1)}, bf16[1,128,768]{2,1,0:T(8,128)(2,1)S(1)}, bf16[1,128,768]{2,1,0:T(8,128)(2,1)S(1)}, bf16[1,128,768]{2,1,0:T(8,128)(2,1)S(1)}, f32[12,257]{1,0:T(8,128)S(1)}) custom-call(s32[1]{0:T(128)S(6)} %copy.11.length_ref, f32[12,257]{1,0:T(8,128)} %bias_hbm.1, bf16[1,128,768]{2,1,0:T(8,128)(2,1)} %query_hbm.1, ...), custom_call_target="tpu_custom_call" | custom-call | tf_op jit(solution)/shard_map/pallas_call | solution.py:404
  32.8 0.9 %shard_map.102 = (bf16[1,128,768]{2,1,0:T(8,128)(2,1)}, bf16[1,128,768]{2,1,0:T(8,128)(2,1)}, bf16[1,128,768]{2,1,0:T(8,128)(2,1)}, bf16[1,128,768]{2,1,0:T(8,128)(2,1)}, f32[12,257]{1,0:T(8,128)}) custom-call(bf16[1,128,768]{2,1,0:T(8,128)(2,1)S(1)} %get-tuple-element.10.refs_0_, bf16[1,128,768]{2,1,0:T(8,128)(2,1)S(1)} %get-tuple-element.11.refs_1_, ...), custom_call_target="tpu_custom_call" | custom-call | tf_op jit(solution)/shard_map/pallas_call | solution.py:434

commit v4 on v3

--- a/solution.py
+++ b/solution.py
@@ -283,52 +283,43 @@
         for side in (0, 1):
             when_side(side, lambda: back_copy(side, tile).start())
 
-    per_chunk = chunk_lanes // lane_tile
-    tiles = chunks * per_chunk
-    held = None
-    for chunk in range(chunks):
-        for array in (0, 1):
-            for side in (0, 1):
-                when_side(side, lambda: rim_copy(side, array, chunk).wait_recv())
-        done = []
-        for tile in range(chunk * per_chunk, (chunk + 1) * per_chunk):
-            fresh = softmax_part(tile)
-            if held is not None:
-                product_part(tile - 1, held)
-                done.append(tile - 1)
-            held = fresh
-        for tile in done:
-            give_back(tile)
-
-    folded = diag_sums[...]
-    for bit in (1, 2, 4):
-        moved = pltpu.roll(folded, extended - bit, 1)
-        folded = jnp.where((turn & bit) != 0, moved, folded)
-    table = jnp.sum(folded.reshape(heads, 8, extended), axis=1)
-
-    def table_copy(level, base, slot_from, slot_to, device):
+    def table_copy(part, base, slot_from, slot_to, device):
         return pltpu.make_async_remote_copy(
-            src_ref=tables.at[base + slot_from],
-            dst_ref=tables.at[base + slot_from],
-            send_sem=table_send_sem.at[base + slot_to],
-            recv_sem=table_recv_sem.at[base + slot_from],
+            src_ref=tables.at[part, base + slot_from],
+            dst_ref=tables.at[part, base + slot_from],
+            send_sem=table_send_sem.at[part, base + slot_to],
+            recv_sem=table_recv_sem.at[part, base + slot_from],
             device_id=device(slot_to),
             device_id_type=MESH,
         )
 
-    def send_tables(level, base, table):
+    parts = [(0, 8), (8, heads - 8)]
+
+    def part_table(part):
+        low_head, count = parts[part]
+        folded = diag_sums[pl.ds(low_head * 8, count * 8), :]
+        turn = lax.broadcasted_iota(jnp.int32, folded.shape, 0) & 7
+        for bit in (1, 2, 4):
+            moved = pltpu.roll(folded, extended - bit, 1)
+            folded = jnp.where((turn & bit) != 0, moved, folded)
+        return jnp.sum(folded.reshape(count, 8, extended), axis=1)
+
+    def send_tables(part, level, table):
         mine, others, device, total = groups[level]
-        tables[base + mine, pl.ds(0, heads), :] = table
+        base = bases[level]
+        tables[part, base + mine, pl.ds(0, parts[part][1]), :] = table
         for slot in others:
-            table_copy(level, base, mine, slot, device).start()
-
-    def sum_tables(level, base):
+            table_copy(part, base, mine, slot, device).start()
+
+    def sum_tables(part, level):
         mine, others, device, total = groups[level]
+        base = bases[level]
         for slot in others:
-            table_copy(level, base, slot, slot, device).wait_recv()
-        whole = tables[base, pl.ds(0, heads), :]
+            table_copy(part, base, slot, slot, device).wait_recv()
+        count = parts[part][1]
+        whole = tables[part, base, pl.ds(0, count), :]
         for slot in range(1, total):
-            whole = whole + tables[base + slot, pl.ds(0, heads), :]
+            whole = whole + tables[part, base + slot, pl.ds(0, count), :]
         return whole
 
     bases = []
@@ -336,6 +327,25 @@
     for mine, others, device, total in groups:
         bases.append(used)
         used += total
+
+    tiles = chunks
+    early = parts[0][1] // per_tile
+    held = None
+    for tile in range(tiles):
+        for array in (0, 1):
+            for side in (0, 1):
+                when_side(side, lambda: rim_copy(side, array, tile).wait_recv())
+        fresh = softmax_part(tile)
+        if held is not None:
+            product_part(tile - 1, held)
+            give_back(tile - 1)
+        held = fresh
+        if tile == early - 1:
+            send_tables(0, 0, part_table(0))
+
+    send_tables(1, 0, part_table(1))
+    product_part(tiles - 1, held)
+    give_back(tiles - 1)
 
     def finish_keys():
         for tile in range(tiles):
@@ -354,26 +364,31 @@
         store(2, staged.at[2], dkey_hbm.at[0])
         store(3, staged.at[3], dvalue_hbm.at[0])
 
-    send_tables(0, bases[0], table)
-    product_part(tiles - 1, held)
-    give_back(tiles - 1)
     store(0, staged.at[0], context_hbm.at[0])
     store(1, staged.at[1], dquery_hbm.at[0])
-    table = sum_tables(0, bases[0])
+    totals = []
+    for part in (0, 1):
+        totals.append(sum_tables(part, 0))
+        if len(groups) > 1:
+            send_tables(part, 1, totals[part])
     for level in range(1, len(groups)):
-        send_tables(level, bases[level], table)
         if level == 1:
             finish_keys()
-        table = sum_tables(level, bases[level])
+        for part in (0, 1):
+            totals[part] = sum_tables(part, level)
+            if level + 1 < len(groups):
+                send_tables(part, level + 1, totals[part])
     if len(groups) == 1:
         finish_keys()
-    bias_rows[pl.ds(0, heads), :] = table
+    for (low_head, count), total_rows in zip(parts, totals):
+        bias_rows[pl.ds(low_head, count), :] = total_rows
     bias_ref[...] = mirrored(bias_rows[...])[:heads, :span]
     store(4, bias_ref, dbias_hbm)
 
     for level, (mine, others, device, total) in enumerate(groups):
         for slot in others:
-            table_copy(level, bases[level], mine, slot, device).wait_send()
+            for part in (0, 1):
+                table_copy(part, bases[level], mine, slot, device).wait_send()
     for side in (0, 1):
         for tile in range(tiles):
             when_side(side, lambda: back_copy(side, tile).wait_send())
@@ -389,7 +404,7 @@
     heads, span = rel_bias.shape
     head_size = width // heads
     extended = 3 * frames
-    chunk_lanes = 2 * lane_tile
+    chunk_lanes = lane_tile
     chunks = width // chunk_lanes
     slots = sum(size * (n_dp if with_dp else 1) for _, size, with_dp in sum_stages(n_dp, n_tm))
     plan = (n_dp, n_tm, heads, frames, head_size, span, chunks, chunk_lanes)
@@ -417,15 +432,15 @@
             pltpu.VMEM((2, tiles, 2, frames, lane_tile), low),
             pltpu.VMEM((2, tiles, 2, frames, lane_tile), low),
             pltpu.VMEM((heads * 8, extended), jnp.float32),
-            pltpu.VMEM((slots, padded_heads, extended), jnp.float32),
+            pltpu.VMEM((2, slots, 8, extended), jnp.float32),
             pltpu.SemaphoreType.DMA((5,)),
             pltpu.SemaphoreType.DMA((5,)),
             pltpu.SemaphoreType.DMA((2, 2, chunks)),
             pltpu.SemaphoreType.DMA((2, 2, chunks)),
             pltpu.SemaphoreType.DMA((2, tiles)),
             pltpu.SemaphoreType.DMA((2, tiles)),
-            pltpu.SemaphoreType.DMA((slots,)),
-            pltpu.SemaphoreType.DMA((slots,)),
+            pltpu.SemaphoreType.DMA((2, slots)),
+            pltpu.SemaphoreType.DMA((2, slots)),
         ],
         compiler_params=pltpu.CompilerParams(
             collective_id=0, has_side_effects=True, vmem_limit_bytes=60 * 1024 * 1024

time: 33.9 us -> 33.5 us (0.988)
  Pallas kernels: 32.5 us -> 32 us
    pallas_call x1, Pallas kernels: 31.5 us -> 31.1 us  [on_device(): pl.pallas_call(functools.partial(kernel, plan), out_shape=held_shapes, in...]
where the time goes in v4:
time: 33.5 us; the launch traced here: 33.3 us
  Pallas kernels  32 us (96%)
  between operations  1.29 us (4%)
    pallas_call x1, Pallas kernels, on_device(): pl.pallas_call(functools.partial(kernel, plan), out_shape=held_shapes, in...  31.1 us
    pallas_call x1, Pallas kernels, on_device(): pl.pallas_call(hand_over, out_shape=shapes, in_specs=[anywhere] * 5, out_...  0.92 us

profile of v4, /device:TPU:0, one launch (start us, length us, event | category | flops | bytes accessed | tf_op | source)
XLA Modules:
  0.0 33.3 jit_solution(5388593141032794819)
XLA Ops:
  1.3 31.1 %shard_map.101 = (bf16[1,128,768]{2,1,0:T(8,128)(2,1)S(1)}, bf16[1,128,768]{2,1,0:T(8,128)(2,1)S(1)}, bf16[1,128,768]{2,1,0:T(8,128)(2,1)S(1)}, bf16[1,128,768]{2,1,0:T(8,128)(2,1)S(1)}, f32[12,257]{1,0:T(8,128)S(1)}) custom-call(s32[1]{0:T(128)S(6)} %copy.11.length_ref, f32[12,257]{1,0:T(8,128)} %bias_hbm.1, bf16[1,128,768]{2,1,0:T(8,128)(2,1)} %query_hbm.1, ...), custom_call_target="tpu_custom_call" | custom-call | tf_op jit(solution)/shard_map/pallas_call | solution.py:419
  32.4 0.9 %shard_map.102 = (bf16[1,128,768]{2,1,0:T(8,128)(2,1)}, bf16[1,128,768]{2,1,0:T(8,128)(2,1)}, bf16[1,128,768]{2,1,0:T(8,128)(2,1)}, bf16[1,128,768]{2,1,0:T(8,128)(2,1)}, f32[12,257]{1,0:T(8,128)}) custom-call(bf16[1,128,768]{2,1,0:T(8,128)(2,1)S(1)} %get-tuple-element.10.refs_0_, bf16[1,128,768]{2,1,0:T(8,128)(2,1)S(1)} %get-tuple-element.11.refs_1_, ...), custom_call_target="tpu_custom_call" | custom-call | tf_op jit(solution)/shard_map/pallas_call | solution.py:449
